TPU v7x, 256 devices: a whole 4x4x8 slice. The times are simulated.
256 devices in a mesh: head: 4 (over y), inner: 2 (over z_lo), outer: 32 (over z_hi, x, core).
Axes of the slice: x: 4, y: 4, z: 8 (z_hi: 4, z_lo: 2; z = z_hi * 2 + z_lo), core: 2. Of those that a mesh axis runs over, the one named last changes fastest.
Arguments:
- queries: bfloat16 [8192, 2048], P(('head', 'inner', 'outer')), may hold values from -2 to 2
- keys: bfloat16 [8192, 512], P(('head', 'inner', 'outer')), may hold values from -2 to 2
- values: bfloat16 [8192, 512], P(('head', 'inner', 'outer')), may hold values from -6 to 6
- out_grad: bfloat16 [8192, 2048], P(('head', 'inner', 'outer')), may hold values from -6 to 6
- span_order: int32 [256], replicated, may hold values from 0 to 255, each once
Outputs:
- query_grad: bfloat16 [8192, 2048], P(('head', 'inner', 'outer'))
- key_grad: bfloat16 [8192, 512], P(('head', 'inner', 'outer'))
- value_grad: bfloat16 [8192, 512], P(('head', 'inner', 'outer'))
Inputs may be any that keep to these rules, and one draw needn't show every extreme that they name: span_order is a permutation of 0 to 255.
All inputs are finite; a program needn't handle non-finite values.
Results may differ from a plain program's by a relative error of at most 0.005.
Values may be sent and summed in bfloat16 or wider, within the bound.
A program may use at most 64 MiB of HBM per device.

v0:
```python
import math

import jax
import jax.numpy as jnp
from jax import lax
from jax.sharding import PartitionSpec as P

D_HEAD = 128


def passed_along(value, axis, steps):
    count = lax.axis_size(axis)
    pairs = [(source, (source + steps) % count) for source in range(count)]
    return lax.ppermute(value, axis, pairs)


def unit_places(span_order, owners, ctx_count, head_count, unit):
    units = jnp.arange(head_count, dtype=jnp.int32)[None, :] * ctx_count + owners[:, None]
    starts = jnp.take(span_order, units.reshape(-1)) * unit
    offsets = jnp.arange(unit, dtype=jnp.int32)
    return (starts[:, None] + offsets[None, :]).reshape(-1)


def row_places(span_order, first, count, rows, ctx_count, unit):
    index = first + jnp.arange(count, dtype=jnp.int32)
    owner = index // rows
    within = index % rows
    units = within // unit * ctx_count + owner
    return jnp.take(span_order, units) * unit + within % unit


def tile_terms(query_tile, grad_tile, key_tile, value_tile, query_places, key_places, scale):
    scores = (
        jnp.einsum("ikgd,jkd->kgij", query_tile, key_tile, preferred_element_type=jnp.float32)
        * scale
    )
    prob_grads = jnp.einsum(
        "ikgd,jkd->kgij", grad_tile, value_tile, preferred_element_type=jnp.float32
    )
    allowed = key_places[None, :] <= query_places[:, None]
    raised = jnp.where(allowed[None, None], jnp.exp(scores), 0.0)
    return (raised, prob_grads)


def body(queries, keys, values, out_grad, span_order):
    head_count = lax.axis_size("head")
    ctx_count = lax.axis_size(("inner", "outer"))
    ctx_index = lax.axis_index(("inner", "outer"))
    unit = queries.shape[0]
    scale = 1.0 / math.sqrt(D_HEAD)
    local_q, local_k, local_v, local_grad = (
        lax.all_to_all(queries, "head", split_axis=1, concat_axis=0, tiled=True),
        lax.all_to_all(keys, "head", split_axis=1, concat_axis=0, tiled=True),
        lax.all_to_all(values, "head", split_axis=1, concat_axis=0, tiled=True),
        lax.all_to_all(out_grad, "head", split_axis=1, concat_axis=0, tiled=True),
    )
    rows = local_q.shape[0]
    kv_local = local_k.shape[1] // D_HEAD
    group = local_q.shape[1] // local_k.shape[1]
    query_tile = local_q.reshape(rows, kv_local, group, D_HEAD)
    grad_tile = local_grad.reshape(rows, kv_local, group, D_HEAD)
    own_ids = jnp.reshape(ctx_index, (1,))
    query_places = unit_places(span_order, own_ids, ctx_count, head_count, unit)
    stat_zero = jnp.zeros((kv_local, group, rows), jnp.float32)
    key_piece = lax.all_gather(local_k, ("inner", "outer"), axis=0, tiled=True)
    value_piece = lax.all_gather(local_v, ("inner", "outer"), axis=0, tiled=True)
    count = key_piece.shape[0]
    width = math.gcd(count, 512)

    def one_block(index, sums):
        offset = index * width
        key_block = lax.dynamic_slice_in_dim(key_piece, offset, width, 0).reshape(
            width, kv_local, D_HEAD
        )
        value_block = lax.dynamic_slice_in_dim(value_piece, offset, width, 0).reshape(
            width, kv_local, D_HEAD
        )
        key_places = row_places(span_order, offset, width, rows, ctx_count, unit)
        raised, prob_grads = tile_terms(
            query_tile, grad_tile, key_block, value_block, query_places, key_places, scale
        )
        return (sums[0] + jnp.sum(raised, axis=3), sums[1] + jnp.sum(raised * prob_grads, axis=3))

    norms, weighted = lax.fori_loop(0, count // width, one_block, (stat_zero, stat_zero))
    deltas = weighted / norms

    def add_tile(query_sum, key_rows, value_rows, key_places):
        count = key_rows.shape[0]
        key_block = key_rows.reshape(count, kv_local, D_HEAD)
        value_block = value_rows.reshape(count, kv_local, D_HEAD)
        raised, prob_grads = tile_terms(
            query_tile, grad_tile, key_block, value_block, query_places, key_places, scale
        )
        weights = raised / norms[..., None]
        probs = weights.astype(jnp.bfloat16)
        slopes = (weights * (prob_grads - deltas[..., None])).astype(jnp.bfloat16)
        query_sum = query_sum + jnp.einsum(
            "kgij,jkd->ikgd", slopes, key_block, preferred_element_type=jnp.float32
        )
        key_term = jnp.einsum(
            "kgij,ikgd->jkd", slopes, query_tile, preferred_element_type=jnp.float32
        ).reshape(count, -1)
        value_term = jnp.einsum(
            "kgij,ikgd->jkd", probs, grad_tile, preferred_element_type=jnp.float32
        ).reshape(count, -1)
        return (query_sum, key_term, value_term)

    query_zero = jnp.zeros((rows, kv_local, group, D_HEAD), jnp.float32)

    def flat_turn(step, state):
        query_sum, key_rows, value_rows, key_sum, value_sum = state
        owner = (ctx_index - step) % ctx_count
        owners = jnp.reshape(owner, (1,))
        key_places = unit_places(span_order, owners, ctx_count, head_count, unit)
        query_sum, key_term, value_term = add_tile(query_sum, key_rows, value_rows, key_places)
        key_sum, value_sum = passed_along(
            (key_sum + key_term, value_sum + value_term), ("inner", "outer"), 1
        )
        key_rows, value_rows = passed_along((key_rows, value_rows), ("inner", "outer"), 1)
        return (query_sum, key_rows, value_rows, key_sum, value_sum)

    grad_zero = jnp.zeros(local_k.shape, jnp.float32)
    final = lax.fori_loop(
        0, ctx_count, flat_turn, (query_zero, local_k, local_v, grad_zero, grad_zero)
    )
    query_sum = final[0]
    key_total = final[3]
    value_total = final[4]
    query_out = (query_sum * scale).astype(jnp.bfloat16).reshape(rows, -1)
    key_out = (key_total * scale).astype(jnp.bfloat16)
    value_out = value_total.astype(jnp.bfloat16)
    return (
        lax.all_to_all(query_out, "head", split_axis=0, concat_axis=1, tiled=True),
        lax.all_to_all(key_out, "head", split_axis=0, concat_axis=1, tiled=True),
        lax.all_to_all(value_out, "head", split_axis=0, concat_axis=1, tiled=True),
    )


def solution(mesh):
    in_specs = (
        P(("head", "inner", "outer"), None),
        P(("head", "inner", "outer"), None),
        P(("head", "inner", "outer"), None),
        P(("head", "inner", "outer"), None),
        P(),
    )
    out_specs = (
        P(("head", "inner", "outer"), None),
        P(("head", "inner", "outer"), None),
        P(("head", "inner", "outer"), None),
    )
    return jax.shard_map(body, mesh=mesh, in_specs=in_specs, out_specs=out_specs, check_vma=False)
```

profile of v0, /device:TPU:32, one launch (start us, length us, event | category | flops | bytes accessed | tf_op | source)
XLA Modules:
  0.0 1143.9 jit_solution(3089267494597623906)
XLA Ops:
  7.9 9.8 all_to_all.127
  18.6 8.5 all_to_all.128
  47.3 85.1 %all-gather.3.cloned.1.call-done = bf16[8192,128]{1,0:T(8,128)(2,1)} async-done(((bf16[128,128]{1,0:T(8,128)(2,1)}), bf16[8192,128]{1,0:T(8,128)(2,1)}) %all-gather.3.cloned.1.call-update) | async-done | bytes 2097168 | tf_op jit(solution)/shard_map/all_gather | solution.py:65
  132.4 114.3 %all-gather.5.cloned.1.call-done = bf16[8192,128]{1,0:T(8,128)(2,1)} async-done(((bf16[128,128]{1,0:T(8,128)(2,1)}), bf16[8192,128]{1,0:T(8,128)(2,1)}) %all-gather.5.cloned.1.call-update) | async-done | bytes 2097168 | tf_op jit(solution)/shard_map/all_gather | solution.py:66
  246.7 103.3 %while.43 = (s32[]{:T(128)}, f32[1,4,128]{2,1,0:T(4,128)S(1)}, f32[1,4,128]{2,1,0:T(4,128)S(1)}, s32[256]{0:T(256)S(1)}, bf16[8192,128]{1,0:T(8,128)(2,1)}, /*in...) while((s32[]{:T(128)}, f32[1,4,128]{2,1,0:T(4,128)S(1)}, ...), condition=%wide.region_3.5_spmd.clone, body=%wide.region_0.4_spmd.clone.sunk | while | flops 135642240 | bytes 2791637 | solution.py:84
  350.1 758.1 %while.44 = (s32[]{:T(128)}, f32[128,1,4,128]{3,0,2,1:T(8,128)S(1)}, bf16[128,128]{1,0:T(8,128)(2,1)S(1)}, bf16[128,128]{1,0:T(8,128)(2,1)S(1)}, f32[128,128]{1,...) while((s32[]{:T(128)}, ...), condition=%wide.region_5.7_spmd.clone, body=%wide.region_4.6_spmd.clone.sunk | while | flops 84526408 | bytes 3551832 | solution.py:123
  366.1 6.1 collective-permute-done
  377.7 6.0 collective-permute-done
  389.2 6.1 collective-permute-done
  400.7 6.1 collective-permute-done
  413.0 6.8 collective-permute-done
  425.8 6.6 collective-permute-done
  437.2 6.0 collective-permute-done
  448.6 6.0 collective-permute-done
  460.1 6.0 collective-permute-done
  472.3 6.0 collective-permute-done
  484.6 6.1 collective-permute-done
  496.3 6.0 collective-permute-done
  507.8 6.0 collective-permute-done
  519.3 6.0 collective-permute-done
  530.8 6.1 collective-permute-done
  542.3 6.1 collective-permute-done
  554.3 6.0 collective-permute-done
  565.7 6.0 collective-permute-done
  577.1 6.1 collective-permute-done
  588.6 6.0 collective-permute-done
  600.1 6.0 collective-permute-done
  611.6 6.0 collective-permute-done
  623.1 6.1 collective-permute-done
  634.6 6.0 collective-permute-done
  646.2 6.0 collective-permute-done
  669.2 6.0 collective-permute-done
  681.3 6.1 collective-permute-done
  693.4 6.1 collective-permute-done
  705.4 6.2 collective-permute-done
  716.8 6.1 collective-permute-done
  728.4 6.1 collective-permute-done
  740.0 6.4 collective-permute-done
  765.6 6.6 collective-permute-done
  777.1 6.9 collective-permute-done
  788.5 7.4 collective-permute-done
  800.1 6.1 collective-permute-done
  811.8 6.0 collective-permute-done
  823.6 6.1 collective-permute-done
  836.3 7.2 collective-permute-done
  847.7 6.1 collective-permute-done
  860.2 6.0 collective-permute-done
  872.6 6.0 collective-permute-done
  885.5 6.0 collective-permute-done
  910.5 6.8 collective-permute-done
  922.0 6.0 collective-permute-done
  933.5 6.0 collective-permute-done
  945.0 6.0 collective-permute-done
  956.4 6.7 collective-permute-done
  967.8 6.1 collective-permute-done
  1005.5 6.0 collective-permute-done
  1018.3 6.0 collective-permute-done
  1030.6 6.8 collective-permute-done
  1042.0 6.1 collective-permute-done
  1053.5 6.0 collective-permute-done
  1065.0 6.0 collective-permute-done
  1076.4 6.0 collective-permute-done
  1087.8 6.0 collective-permute-done
  1099.2 6.0 collective-permute-done
  (1686 shorter events, 544.2 us)
Async XLA Ops:
  7.2 125.2 %all-gather.3.cloned.1.call-start = ((), (), s32[]{:S(2)}) async-start(), calls=%async_computation.7 | async-start | bytes 2129920 | tf_op jit(solution)/shard_map/all_gather | solution.py:65
  17.8 228.9 %all-gather.5.cloned.1.call-start = ((), (), s32[]{:S(2)}) async-start(), calls=%async_computation.8 | async-start | bytes 2129920 | tf_op jit(solution)/shard_map/all_gather | solution.py:66
  353.6 10.0 collective-permute-start.3
  363.6 10.2 collective-permute-start.1
  365.7 9.5 collective-permute-start.3
  388.8 9.5 collective-permute-start.3
  400.4 10.2 collective-permute-start.3
  410.5 9.6 collective-permute-start.1
  412.3 10.0 collective-permute-start.2
  412.6 10.7 collective-permute-start.3
  459.7 10.1 collective-permute-start.3
  471.9 10.2 collective-permute-start.3
  484.3 9.6 collective-permute-start.3
  519.0 9.4 collective-permute-start.3
  530.5 9.4 collective-permute-start.3
  541.7 9.5 collective-permute-start.2
  542.0 9.9 collective-permute-start.3
  588.3 9.4 collective-permute-start.3
  611.3 9.4 collective-permute-start.3
  634.3 9.4 collective-permute-start.3
  645.8 9.4 collective-permute-start.3
  668.8 10.0 collective-permute-start.3
  680.9 10.0 collective-permute-start.3
  692.8 9.5 collective-permute-start.2
  693.0 9.9 collective-permute-start.3
  716.4 9.5 collective-permute-start.3
  728.0 9.5 collective-permute-start.3
  739.6 10.7 collective-permute-start.3
  752.2 10.2 collective-permute-start.2
  752.4 10.7 collective-permute-start.3
  774.6 9.7 collective-permute-start.1
  786.0 9.9 collective-permute-start
  786.0 10.2 collective-permute-start.1
  788.1 9.6 collective-permute-start.3
  797.7 10.2 collective-permute-start.1
  799.8 9.6 collective-permute-start.3
  811.4 9.7 collective-permute-start.3
  823.0 10.1 collective-permute-start.2
  823.3 10.6 collective-permute-start.3
  833.8 9.6 collective-permute-start
  833.8 10.0 collective-permute-start.1
  847.0 10.0 collective-permute-start.2
  847.3 10.4 collective-permute-start.3
  859.8 10.3 collective-permute-start.3
  872.0 10.3 collective-permute-start.2
  872.2 10.8 collective-permute-start.3
  884.9 10.3 collective-permute-start.2
  885.1 10.7 collective-permute-start.3
  897.7 9.7 collective-permute-start.2
  897.9 10.1 collective-permute-start.3
  908.1 9.6 collective-permute-start.1
  954.0 9.4 collective-permute-start.1
  965.4 9.6 collective-permute-start.1
  967.2 9.5 collective-permute-start.2
  967.4 9.9 collective-permute-start.3
  979.5 10.7 collective-permute-start.3
  992.0 9.6 collective-permute-start.2
  992.3 10.8 collective-permute-start.3
  1004.9 10.3 collective-permute-start.2
  1005.2 10.7 collective-permute-start.3
  1017.7 9.8 collective-permute-start.2
  1018.0 10.2 collective-permute-start.3
  1028.2 9.5 collective-permute-start.1
  1108.8 9.6 all-to-all-start.6
  (203 other events, 2212.5 us)
Sparse Core Ops, SparseCore 0:
  17.9 114.4 all-gather.2
  134.2 112.3 all-gather.4
where the time goes:
time: 1150 us; the launch traced here: 1140 us
  waiting for transfers between devices  823 us (72%)
  local copies, waits for them, and re-layouts  119 us (10%)
  matrix products  103 us (9%)
  starting transfers between devices  35.3 us (3%)
  other arithmetic  22.5 us (2%)
  blocking collectives  18.3 us (2%)
  between operations  14.2 us (1%)
    ppermute x256, waiting for transfers between devices, passed_along(): return lax.ppermute(value, axis, pairs)  601 us
    all_gather x1, waiting for transfers between devices, body(): lax.all_gather(local_v, ('inner', 'outer'), axis=0, tiled=True)  114 us
    all_gather x1, waiting for transfers between devices, body(): key_piece = lax.all_gather(local_k, ('inner', 'outer'), axis=0, tiled=True)  85.1 us
    gather x16, local copies, waits for them, and re-layouts, row_places(): return jnp.take(span_order, units) * unit + within % unit  56.3 us
    gather x65, local copies, waits for them, and re-layouts, unit_places(): starts = jnp.take(span_order, units.reshape(-1)) * unit  42.3 us
    dot_general x80, matrix products, tile_terms(): jnp.einsum('ikgd,jkd->kgij', query_tile, key_tile, preferred_element_type...  33.7 us
    dot_general x80, matrix products, tile_terms(): jnp.einsum('ikgd,jkd->kgij', grad_tile, value_tile, preferred_element_typ...  31.8 us
  transfers between devices with their start and end apart: 263, of which 263 were waited for; matrix products, arithmetic and copies ran while one was open for 12% of the time, Pallas kernels for 0%

commit v1 on v0

v1 whole, which is shorter than its diff:
```python
import math

import jax
import jax.numpy as jnp
from jax import lax
from jax.experimental import pallas as pl
from jax.experimental.pallas import tpu as pltpu
from jax.sharding import PartitionSpec as P

MESH = pl.DeviceIdType.MESH
D = 128
G = 4
NY, NZ, NX, NC = 4, 8, 4, 2
U = 32
C = NY * U
QR = NX * C
KB = NC * C
GD = G * D
F32, BF16 = jnp.float32, jnp.bfloat16
SCALE = 1.0 / math.sqrt(D)
LOG2E = 1.4426950408889634
NT = (((1,), (1,)), ((), ()))
NN = (((1,), (0,)), ((), ()))


def dot(a, b, dims):
    return lax.dot_general(a, b, dims, preferred_element_type=F32)


def kernel(
    span, q_in, k_in, v_in, g_in, q_out, k_out, v_out,
    qg, kv, kt, es, ds, qp, nsum, wsum, stat, total, dqt, dkv, sib_in, z_out, z_in,
    dq_out, dq_in, q_fin, kv_fin,
    loc_sem, y_send, y_recv, x_send, x_recv, z_send, z_recv, c_send, c_recv,
    st_send, st_recv, dc_send, dc_recv, dz_send, dz_recv, dx_send, dx_recv, o_send, o_recv,
):
    y, zl, o = lax.axis_index("head"), lax.axis_index("inner"), lax.axis_index("outer")
    zh, x, c = o // (NX * NC), (o // NC) % NX, o % NC
    z = zh * 2 + zl

    def dev(y, z, x, c):
        return (y, z % 2, ((z // 2) * NX + x) * NC + c)

    def up(value, count, step):
        return (value + step + count) % count

    def copy(src, dst, send, recv, device):
        return pltpu.make_async_remote_copy(
            src_ref=src, dst_ref=dst, send_sem=send, recv_sem=recv, device_id=device, device_id_type=MESH
        )

    def y_dev(s):
        return dev(up(y, NY, s), z, x, c)

    def x_dev(s):
        return dev(y, z, up(x, NX, s), c)

    def z_dev(s):
        return dev(y, up(z, NZ, s), x, c)

    c_dev = dev(y, z, x, 1 - c)

    q_rows = pl.ds(pl.multiple_of(x * C + y * U, U), U)
    k_rows = pl.ds(pl.multiple_of((z * NC + c) * C + y * U, U), U)

    def pieces(to):
        wide = pl.ds(pl.multiple_of(to * GD, GD), GD)
        thin = pl.ds(pl.multiple_of(to * D, D), D)
        return (
            (q_in.at[:, wide], qg.at[q_rows, pl.ds(0, GD)]),
            (g_in.at[:, wide], qg.at[q_rows, pl.ds(GD, GD)]),
            (k_in.at[:, thin], kv.at[k_rows, pl.ds(0, D)]),
            (v_in.at[:, thin], kv.at[k_rows, pl.ds(D, D)]),
        )

    own = [pltpu.make_async_copy(a, b, loc_sem.at[i]) for i, (a, b) in enumerate(pieces(y))]
    for one in own:
        one.start()

    barrier = pltpu.get_barrier_semaphore()
    partners = (
        [y_dev(s) for s in range(1, NY)] + [x_dev(s) for s in range(1, NX)]
        + [z_dev(s) for s in range(1, NZ)] + [c_dev]
    )
    for device in partners:
        pl.semaphore_signal(barrier, inc=1, device_id=device, device_id_type=MESH)
    pl.semaphore_wait(barrier, len(partners))

    sends = []
    for s in range(1, NY):
        for i, (a, b) in enumerate(pieces(up(y, NY, s))):
            sends.append(copy(a, b, y_send.at[s - 1, i], y_recv.at[s - 1, i], y_dev(s)))
    for one in sends:
        one.start()

    lane = lax.broadcasted_iota(jnp.int32, (8, QR), 1)
    places = jnp.zeros((8, QR), jnp.int32)
    for xx in range(NX):
        for yy in range(NY):
            unit = yy * (NZ * NX * NC) + zl * (NZ // 2 * NX * NC) + (zh * NX + xx) * NC + c
            places = jnp.where(lane // U == xx * NY + yy, span[unit] * U, places)
    qp[...] = places + lane % U
    nsum[...] = jnp.zeros_like(nsum)
    wsum[...] = jnp.zeros_like(wsum)
    dqt[...] = jnp.zeros_like(dqt)

    for one in own:
        one.wait()
    for one in sends:
        one.wait_recv()

    def q_part(s, cols):
        return qg.at[pl.ds(pl.multiple_of(up(x, NX, s) * C, C), C), cols]

    def k_part(s, cols):
        return kv.at[pl.ds(pl.multiple_of((up(z, NZ, s) * NC + c) * C, C), C), cols]

    def q_copy(i, s, cols, to):
        part = q_part(s, cols)
        return copy(part, part, x_send.at[i], x_recv.at[i], x_dev(to))

    def k_copy(i, s, cols, to):
        part = k_part(s, cols)
        return copy(part, part, z_send.at[i], z_recv.at[i], z_dev(to))

    def c_copy(s):
        part = k_part(s, pl.ds(0, 2 * D))
        i = s % NZ
        return copy(part, part, c_send.at[i], c_recv.at[i], c_dev)

    every, low, high = pl.ds(0, 2 * GD), pl.ds(0, GD), pl.ds(GD, GD)
    k_every, k_low, k_high = pl.ds(0, 2 * D), pl.ds(0, D), pl.ds(D, D)
    qs = [q_copy(0, 0, every, 1), q_copy(1, 0, every, -1), q_copy(2, -1, low, 1), q_copy(3, 1, high, -1)]
    ks = []
    for s in range(4):
        a, b = (k_every, k_every) if s < 3 else (k_low, k_high)
        ks += [k_copy(2 * s, -s, a, 1), k_copy(2 * s + 1, s, b, -1)]
    cs = [c_copy(s) for s in (0, -1, 1, -2, 2, -3, 3, 4)]

    ks[0].start()
    ks[1].start()
    qs[0].start()
    qs[1].start()
    cs[0].start()
    for s in range(1, 4):
        ks[2 * s - 2].wait_recv()
        ks[2 * s].start()
        cs[2 * s - 1].start()
        ks[2 * s - 1].wait_recv()
        ks[2 * s + 1].start()
        cs[2 * s].start()
        if s == 2:
            qs[0].wait_recv()
            qs[2].start()
            qs[1].wait_recv()
            qs[3].start()
    ks[6].wait_recv()
    ks[7].wait_recv()
    cs[7].start()
    qs[2].wait_recv()
    qs[3].wait_recv()
    for one in cs:
        one.wait_recv()

    row = lax.broadcasted_iota(jnp.int32, (U, QR), 0)

    def first(b, carry):
        rows = pl.ds(pl.multiple_of(b * KB, KB), KB)
        keys, vals = kv[rows, 0:D], kv[rows, D : 2 * D]
        masks = []
        limit = qp[0:1, :]
        for cc in range(NC):
            for yy in range(NY):
                unit = yy * (NZ * NX * NC) + (b % 2) * (NZ // 2 * NX * NC) + ((b // 2) * NX + x) * NC + cc
                masks.append(row + span[unit] * U <= limit)
        mask = jnp.concatenate(masks, axis=0)
        kt[:, rows] = keys.T
        for h in range(G):
            cols = slice(h * QR, (h + 1) * QR)
            scores = dot(keys, qg[:, h * D : (h + 1) * D], NT)
            raised = jnp.where(mask, jnp.exp2(scores * (SCALE * LOG2E)), 0.0)
            grads = dot(vals, qg[:, GD + h * D : GD + (h + 1) * D], NT)
            es[rows, cols] = raised
            ds[rows, cols] = grads
            nsum[:, cols] += jnp.sum(raised.reshape(KB // 8, 8, QR), axis=0)
            wsum[:, cols] += jnp.sum((raised * grads).reshape(KB // 8, 8, QR), axis=0)
        return carry

    lax.fori_loop(0, NZ, first, 0)

    for h in range(G):
        cols = slice(h * QR, (h + 1) * QR)
        stat[x, h : h + 1, :] = jnp.sum(nsum[:, cols], axis=0, keepdims=True)
        stat[x, G + h : G + h + 1, :] = jnp.sum(wsum[:, cols], axis=0, keepdims=True)
    stats = [
        copy(stat.at[x], stat.at[x], st_send.at[s - 1], st_recv.at[s - 1], x_dev(s)) for s in range(1, NX)
    ]
    for one in stats:
        one.start()
    for one in stats:
        one.wait_recv()
    both = stat[0] + stat[1] + stat[2] + stat[3]
    inverse = 1.0 / both[0:G]
    total[0:G, :] = inverse
    total[G : 2 * G, :] = both[G : 2 * G] * inverse

    def block(t):
        return up(z, NZ, t + 1)

    def half(b, core):
        return pl.ds(pl.multiple_of(b * KB + core * C, C), C)

    def to_sibling(t):
        b = block(t)
        return copy(dkv.at[half(b, 1 - c), :], sib_in.at[b], dc_send.at[t], dc_recv.at[t], c_dev)

    def to_owner(t):
        b = block(t)
        return copy(z_out.at[b], z_in.at[z], dz_send.at[t], dz_recv.at[t], dev(y, b, x, c))

    def finish(t):
        b = block(t)
        to_sibling(t).wait_recv()
        z_out[b] = (dkv[half(b, c), :] + sib_in[b]).astype(BF16)
        to_owner(t).start()

    def second(t, carry):
        b = block(t)
        rows = pl.ds(pl.multiple_of(b * KB, KB), KB)
        key_sum = jnp.zeros((KB, D), F32)
        val_sum = jnp.zeros((KB, D), F32)
        for h in range(G):
            cols = slice(h * QR, (h + 1) * QR)
            weights = es[rows, cols] * total[h : h + 1, :]
            probs = weights.astype(BF16)
            slopes = (weights * (ds[rows, cols] - total[G + h : G + h + 1, :])).astype(BF16)
            val_sum += dot(probs, qg[:, GD + h * D : GD + (h + 1) * D], NN)
            key_sum += dot(slopes, qg[:, h * D : (h + 1) * D], NN)
            dqt[h] += dot(kt[:, rows], slopes, NN)
        dkv[rows, 0:D] = key_sum
        dkv[rows, D : 2 * D] = val_sum
        to_sibling(t).start()

        @pl.when(t > 0)
        def _():
            finish(t - 1)

        return carry

    lax.fori_loop(0, NZ, second, 0)

    for h in range(G):
        dq_out[:, h * D : (h + 1) * D] = (dqt[h].T * SCALE).astype(BF16)
    dxs = []
    for s in range(1, NX):
        part = dq_out.at[pl.ds(pl.multiple_of(up(x, NX, s) * C, C), C), :]
        dxs.append(copy(part, dq_in.at[x], dx_send.at[s - 1], dx_recv.at[s - 1], x_dev(s)))
    for one in dxs:
        one.start()
    to_sibling(NZ - 1).wait_recv()
    for one in dxs:
        one.wait_recv()
    q_sum = dq_out[pl.ds(pl.multiple_of(x * C, C), C), :].astype(F32)
    for s in range(1, NX):
        q_sum += dq_in[up(x, NX, s)].astype(F32)
    q_fin[...] = q_sum.astype(BF16)

    wide = pl.ds(pl.multiple_of(y * GD, GD), GD)
    thin = pl.ds(pl.multiple_of(y * D, D), D)

    def results(to):
        rows = pl.ds(pl.multiple_of(to * U, U), U)
        return (
            (q_fin.at[rows, :], q_out.at[:, wide]),
            (kv_fin.at[rows, pl.ds(0, D)], k_out.at[:, thin]),
            (kv_fin.at[rows, pl.ds(D, D)], v_out.at[:, thin]),
        )

    outs = []
    for s in range(1, NY):
        for i, (a, b) in enumerate(results(up(y, NY, s))):
            outs.append((i, copy(a, b, o_send.at[s - 1, i], o_recv.at[s - 1, i], y_dev(s))))
    mine = [(i, pltpu.make_async_copy(a, b, loc_sem.at[i])) for i, (a, b) in enumerate(results(y))]
    for i, one in outs + mine:
        if i == 0:
            one.start()

    for t in range(NZ - 1):
        to_owner(t).wait_recv()
    kv_sum = dkv[half(z, c), :] + sib_in[z]
    for s in range(1, NZ):
        kv_sum += z_in[up(z, NZ, s)].astype(F32)
    kv_fin[:, 0:D] = (kv_sum[:, 0:D] * SCALE).astype(BF16)
    kv_fin[:, D : 2 * D] = kv_sum[:, D : 2 * D].astype(BF16)
    for i, one in outs + mine:
        if i > 0:
            one.start()

    for one in sends + qs + ks + cs + stats + dxs:
        one.wait_send()
    for t in range(NZ):
        to_sibling(t).wait_send()
    for t in range(NZ - 1):
        to_owner(t).wait_send()
    for i, one in outs:
        one.wait()
    for i, one in mine:
        one.wait()


def body(queries, keys, values, out_grad, span_order):
    keys_all = NZ * NC * C
    dma = pltpu.SemaphoreType.DMA
    anywhere = pl.BlockSpec(memory_space=pl.ANY)
    return pl.pallas_call(
        kernel,
        out_shape=(
            jax.ShapeDtypeStruct(queries.shape, BF16),
            jax.ShapeDtypeStruct(keys.shape, BF16),
            jax.ShapeDtypeStruct(values.shape, BF16),
        ),
        in_specs=[pl.BlockSpec(memory_space=pltpu.SMEM)] + [anywhere] * 4,
        out_specs=(anywhere,) * 3,
        scratch_shapes=[
            pltpu.VMEM((QR, 2 * GD), BF16),
            pltpu.VMEM((keys_all, 2 * D), BF16),
            pltpu.VMEM((D, keys_all), BF16),
            pltpu.VMEM((keys_all, G * QR), F32),
            pltpu.VMEM((keys_all, G * QR), F32),
            pltpu.VMEM((8, QR), jnp.int32),
            pltpu.VMEM((8, G * QR), F32),
            pltpu.VMEM((8, G * QR), F32),
            pltpu.VMEM((NX, 2 * G, QR), F32),
            pltpu.VMEM((2 * G, QR), F32),
            pltpu.VMEM((G, D, QR), F32),
            pltpu.VMEM((keys_all, 2 * D), F32),
            pltpu.VMEM((NZ, C, 2 * D), F32),
            pltpu.VMEM((NZ, C, 2 * D), BF16),
            pltpu.VMEM((NZ, C, 2 * D), BF16),
            pltpu.VMEM((QR, GD), BF16),
            pltpu.VMEM((NX, C, GD), BF16),
            pltpu.VMEM((C, GD), BF16),
            pltpu.VMEM((C, 2 * D), BF16),
            dma((4,)),
            dma((NY - 1, 4)), dma((NY - 1, 4)),
            dma((4,)), dma((4,)),
            dma((8,)), dma((8,)),
            dma((NZ,)), dma((NZ,)),
            dma((NX - 1,)), dma((NX - 1,)),
            dma((NZ,)), dma((NZ,)),
            dma((NZ - 1,)), dma((NZ - 1,)),
            dma((NX - 1,)), dma((NX - 1,)),
            dma((NY - 1, 3)), dma((NY - 1, 3)),
        ],
        compiler_params=pltpu.CompilerParams(
            collective_id=0, has_side_effects=True, vmem_limit_bytes=56 * 2**20
        ),
    )(span_order, queries, keys, values, out_grad)


def solution(mesh):
    rows = P(("head", "inner", "outer"), None)
    return jax.shard_map(
        body,
        mesh=mesh,
        in_specs=(rows, rows, rows, rows, P()),
        out_specs=(rows, rows, rows),
        check_vma=False,
    )
```

time: 1150 us -> 68.6 us (0.06)
  waiting for transfers between devices: 823 us -> 0 us
  local copies, waits for them, and re-layouts: 119 us -> 2.96 us
  matrix products: 103 us -> 0 us
  Pallas kernels: 0 us -> 64.6 us
  starting transfers between devices: 35.3 us -> 0 us
  other arithmetic: 22.5 us -> 0 us
  blocking collectives: 18.3 us -> 0 us
  between operations: 14.2 us -> 0.65 us
    ppermute x256 -> x0, waiting for transfers between devices: 601 us -> none  [passed_along(): return lax.ppermute(value, axis, pairs)]
    all_gather x2 -> x0, waiting for transfers between devices: 199 us -> none  [the longest x1 114 us: body(): lax.all_gather(local_v, ('inner', 'outer'), axis=0, tiled=True)]
    dot_general x352 -> x0, matrix products: 103 us -> none  [the longest x80 33.7 us: tile_terms(): jnp.einsum('ikgd,jkd->kgij', query_tile, key_tile, preferred_element_type...]
    gather x81 -> x0, local copies, waits for them, and re-layouts: 98.6 us -> none  [the longest x16 56.3 us: row_places(): return jnp.take(span_order, units) * unit + within % unit]
    pallas_call x0 -> x1, Pallas kernels: none -> 64.6 us  [body(): pl.pallas_call(kernel, out_shape=(jax.ShapeDtypeStruct(queries.shape, BF1...]
    all_to_all x5 -> x0, waiting for transfers between devices: 23 us -> none  [the longest x1 5.83 us: body(): lax.all_to_all(queries, 'head', split_axis=1, concat_axis=0, tiled=True)]
    all_to_all x2 -> x0, blocking collectives: 18.3 us -> none  [the longest x1 9.81 us: body(): lax.all_to_all(keys, 'head', split_axis=1, concat_axis=0, tiled=True)]
    ppermute x256 -> x0, starting transfers between devices: 17.8 us -> none  [passed_along(): return lax.ppermute(value, axis, pairs)]
  transfers between devices with their start and end apart: 263 -> 0, of which waited for: 263 -> 0; matrix products, arithmetic and copies ran while one was open for 12% -> 0% of each run, Pallas kernels for 0% -> 0%
where the time goes in v1:
time: 68.6 us; the launch traced here: 68.3 us
  Pallas kernels  64.6 us (94%)
  local copies, waits for them, and re-layouts  2.96 us (4%)
    pallas_call x1, Pallas kernels, body(): pl.pallas_call(kernel, out_shape=(jax.ShapeDtypeStruct(queries.shape, BF1...  64.6 us
    unnamed x7, local copies, waits for them, and re-layouts  2.96 us

profile of v1, /device:TPU:32, one launch (start us, length us, event | category | flops | bytes accessed | tf_op | source)
XLA Modules:
  0.0 68.3 jit_solution(17361091191069597108)
XLA Ops:
  0.6 64.6 %shard_map.76 = (bf16[32,2048]{1,0:T(8,128)(2,1)}, bf16[32,512]{1,0:T(8,128)(2,1)}, bf16[32,512]{1,0:T(8,128)(2,1)}) custom-call(s32[256]{0:T(256)} %span.1, bf16[32,2048]{1,0:T(8,128)(2,1)} %q_in.1, bf16[32,512]{1,0:T(8,128)(2,1)} %k_in.1, bf16[32,512]{1,0:T(8,128)(2,1)} %v_in.1, bf16[32,2048]{1,0:T(8,128)(2,1)} %g_in.1), custom_call_target="tpu_custom_call" | custom-call | tf_op jit(solution)/shard_map/pallas_call | solution.py:315
  65.3 0.0 copy-start.1
  65.3 1.6 %copy.11 = bf16[32,2048]{1,0:T(8,128)(2,1)} copy(bf16[32,2048]{1,0:T(8,128)(2,1)} %get-tuple-element.6) | data formatting | bytes 262144
  66.9 0.0 copy-done.1
  66.9 0.0 copy-start
  66.9 0.6 copy.12
  67.5 0.2 copy-done
  67.6 0.6 copy.13
Async XLA Ops:
  65.3 1.6 %copy-start.1 = (bf16[32,512]{1,0:T(8,128)(2,1)S(1)}, bf16[32,512]{1,0:T(8,128)(2,1)}, u32[]{:S(2)}) copy-start(bf16[32,512]{1,0:T(8,128)(2,1)} %get-tuple-element.7) | copy-start | bytes 98308
  66.9 0.8 %copy-start = (bf16[32,512]{1,0:T(8,128)(2,1)S(1)}, bf16[32,512]{1,0:T(8,128)(2,1)}, u32[]{:S(2)}) copy-start(bf16[32,512]{1,0:T(8,128)(2,1)} %get-tuple-element.8) | copy-start | bytes 98308

commit v2 on v1

v2 whole, which is shorter than its diff:
```python
import math

import jax
import jax.numpy as jnp
from jax import lax
from jax.experimental import pallas as pl
from jax.experimental.pallas import tpu as pltpu
from jax.sharding import PartitionSpec as P

MESH = pl.DeviceIdType.MESH
D = 128
G = 4
NY, NZ, NX, NC = 4, 8, 4, 2
U = 32
C = NY * U
QR = NX * C
KB = NC * C
GD = G * D
F32, BF16 = jnp.float32, jnp.bfloat16
SCALE = 1.0 / math.sqrt(D)
LOG2E = 1.4426950408889634
NT = (((1,), (1,)), ((), ()))
NN = (((1,), (0,)), ((), ()))
REL = (0, 1, 3, 2)


def dot(a, b, dims):
    return lax.dot_general(a, b, dims, preferred_element_type=F32)


def kernel(
    span, q_in, k_in, v_in, g_in, q_out, k_out, v_out,
    qg, kv, kt, es, ds, qp, nsum, wsum, stat, stat_in, total, dqt, dkv, sib_in, z_out, z_in,
    dq_out, dq_in, q_fin, kv_fin,
    loc_sem, y_send, y_recv, x_send, x_recv, z_send, z_recv, c_send, c_recv,
    st_send, st_recv, dc_send, dc_recv, dz_send, dz_recv, dx_send, dx_recv, o_send, o_recv,
):
    y, zl, o = lax.axis_index("head"), lax.axis_index("inner"), lax.axis_index("outer")
    zh, x, c = o // (NX * NC), (o // NC) % NX, o % NC
    z = zh * 2 + zl

    def dev(y, z, x, c):
        return (y, z % 2, ((z // 2) * NX + x) * NC + c)

    def up(value, count, step):
        return (value + step + count) % count

    def copy(src, dst, send, recv, device):
        return pltpu.make_async_remote_copy(
            src_ref=src, dst_ref=dst, send_sem=send, recv_sem=recv, device_id=device, device_id_type=MESH
        )

    def y_dev(s):
        return dev(up(y, NY, s), z, x, c)

    def x_dev(s):
        return dev(y, z, up(x, NX, s), c)

    def z_dev(s):
        return dev(y, up(z, NZ, s), x, c)

    c_dev = dev(y, z, x, 1 - c)

    def away(p):
        return (p + 1) // 2 * (2 * (p % 2) - 1)

    def pieces(s):
        to, rows = up(y, NY, s), pl.ds((NY - s) % NY * U, U)
        wide = pl.ds(pl.multiple_of(to * GD, GD), GD)
        thin = pl.ds(pl.multiple_of(to * D, D), D)
        return (
            (k_in.at[:, thin], kv.at[rows, pl.ds(0, D)]),
            (v_in.at[:, thin], kv.at[rows, pl.ds(D, D)]),
            (q_in.at[:, wide], qg.at[rows, pl.ds(0, GD)]),
            (g_in.at[:, wide], qg.at[rows, pl.ds(GD, GD)]),
        )

    own = [pltpu.make_async_copy(a, b, loc_sem.at[i]) for i, (a, b) in enumerate(pieces(0))]
    for one in own:
        one.start()

    barrier = pltpu.get_barrier_semaphore()
    partners = (
        [y_dev(s) for s in range(1, NY)] + [x_dev(s) for s in range(1, NX)]
        + [z_dev(s) for s in range(1, NZ)] + [c_dev]
    )
    for device in partners:
        pl.semaphore_signal(barrier, inc=1, device_id=device, device_id_type=MESH)

    lane = lax.broadcasted_iota(jnp.int32, (8, QR), 1)
    places = jnp.zeros((8, QR), jnp.int32)
    for i in range(NX):
        for s in range(NY):
            unit = up(y, NY, s) * (NZ * NX * NC) + zl * (NZ // 2 * NX * NC) + (zh * NX + up(x, NX, REL[i])) * NC + c
            places = jnp.where(lane // U == i * NY + s, span[unit] * U, places)
    qp[...] = places + lane % U
    nsum[...] = jnp.zeros_like(nsum)
    wsum[...] = jnp.zeros_like(wsum)

    for one in own:
        one.wait()
    pl.semaphore_wait(barrier, len(partners))

    ys = {}
    for s in (1, 3, 2):
        for i, (a, b) in enumerate(pieces(s)):
            ys[s, i] = copy(a, b, y_send.at[s - 1, i], y_recv.at[s - 1, i], y_dev(s))
    def x_copy(way, s):
        rows = (NY - s) % NY * U
        slot, to, step, first, width = (
            (0, 2, 1, 0, 2 * GD), (0, 1, -1, 0, 2 * GD), (2, 3, 1, 0, GD), (1, 3, -1, GD, GD),
        )[way]
        return copy(
            qg.at[pl.ds(slot * C + rows, U), pl.ds(first, width)],
            qg.at[pl.ds(to * C + rows, U), pl.ds(first, width)],
            x_send.at[way, s], x_recv.at[way, s], x_dev(step),
        )

    def z_copy(i, slot, to, step, first, width):
        return copy(
            kv.at[pl.ds(slot * KB, C), pl.ds(first, width)],
            kv.at[pl.ds(to * KB, C), pl.ds(first, width)],
            z_send.at[i], z_recv.at[i], z_dev(step),
        )

    def c_copy(p):
        rows, there = p * KB, p * KB + C
        if not isinstance(p, int):
            rows, there = pl.multiple_of(rows, C), pl.multiple_of(there, C)
        return copy(kv.at[pl.ds(rows, C), :], kv.at[pl.ds(there, C), :], c_send.at[p], c_recv.at[p], c_dev)

    xs = {(way, s): x_copy(way, s) for way in range(4) for s in range(NY)}
    zs = {
        2: z_copy(2, 0, 2, 1, 0, 2 * D), 1: z_copy(1, 0, 1, -1, 0, 2 * D),
        4: z_copy(4, 0, 4, 2, 0, 2 * D), 3: z_copy(3, 0, 3, -2, 0, 2 * D),
        6: z_copy(6, 2, 6, 2, 0, 2 * D), 5: z_copy(5, 1, 5, -2, 0, 2 * D),
        7: z_copy(7, 4, 7, 2, 0, D), 8: z_copy(8, 3, 7, -2, D, D),
    }
    order = (0, 1, 3, 2)
    for i in range(2):
        for s in order[1:]:
            ys[s, i].start()
    xs[0, 0].start()
    xs[1, 0].start()
    for s in order[1:]:
        for i in (2, 3):
            ys[s, i].start()

    for s in order[1:]:
        ys[s, 0].wait_recv()
        ys[s, 1].wait_recv()
    for i in (2, 1, 4, 3):
        zs[i].start()
    c_copy(0).start()
    for s in order[1:]:
        ys[s, 2].wait_recv()
        ys[s, 3].wait_recv()
        xs[0, s].start()
        xs[1, s].start()
    for i in (2, 1):
        zs[i].wait_recv()
        zs[i + 4].start()
        c_copy(i).start()
    xs[0, 0].wait_recv()
    xs[2, 0].start()
    xs[1, 0].wait_recv()
    xs[3, 0].start()
    zs[4].wait_recv()
    zs[7].start()
    c_copy(4).start()
    zs[3].wait_recv()
    zs[8].start()
    c_copy(3).start()
    for s in order[1:]:
        xs[0, s].wait_recv()
        xs[2, s].start()
        xs[1, s].wait_recv()
        xs[3, s].start()
    for i in (6, 5):
        zs[i].wait_recv()
        c_copy(i).start()

    row = lax.broadcasted_iota(jnp.int32, (U, 1), 0)

    def tile(p, low, width):
        rows = pl.ds(p * KB if isinstance(p, int) else pl.multiple_of(p * KB, KB), KB)
        keys, vals = kv[rows, 0:D], kv[rows, D : 2 * D]
        masks = []
        limit = jnp.broadcast_to(qp[0:1, low : low + width], (U, width))
        zz = up(z, NZ, away(p))
        for cc in (c, 1 - c):
            for s in range(NY):
                unit = up(y, NY, s) * (NZ * NX * NC) + (zz % 2) * (NZ // 2 * NX * NC) + ((zz // 2) * NX + x) * NC + cc
                masks.append(row + span[unit] * U <= limit)
        mask = jnp.concatenate(masks, axis=0)
        if low == 0:
            kt[:, rows] = keys.T
        for h in range(G):
            cols = slice(h * QR + low, h * QR + low + width)
            scores = dot(keys, qg[low : low + width, h * D : (h + 1) * D], NT)
            raised = jnp.where(mask, jnp.exp2(scores * (SCALE * LOG2E)), 0.0)
            grads = dot(vals, qg[low : low + width, GD + h * D : GD + (h + 1) * D], NT)
            es[rows, cols] = raised
            ds[rows, cols] = grads
            nsum[:, cols] += jnp.sum(raised.reshape(KB // 8, 8, width), axis=0)
            wsum[:, cols] += jnp.sum((raised * grads).reshape(KB // 8, 8, width), axis=0)

    def near(p, carry):
        @pl.when(p > 0)
        def _():
            c_copy(p).wait_recv()

        tile(p, 0, QR // 2)
        return carry

    def far(p, carry):
        tile(p, QR // 2, QR // 2)
        return carry

    c_copy(0).wait_recv()
    lax.fori_loop(0, NZ - 1, near, 0)
    zs[7].wait_recv()
    zs[8].wait_recv()
    c_copy(7).start()
    for s in range(NY):
        xs[2, s].wait_recv()
        xs[3, s].wait_recv()
    lax.fori_loop(0, NZ - 1, far, 0)
    c_copy(7).wait_recv()
    tile(7, 0, QR)

    for h in range(G):
        cols = slice(h * QR, (h + 1) * QR)
        stat[h : h + 1, :] = jnp.sum(nsum[:, cols], axis=0, keepdims=True)
        stat[G + h : G + h + 1, :] = jnp.sum(wsum[:, cols], axis=0, keepdims=True)
    stats = [
        copy(stat, stat_in.at[s - 1], st_send.at[s - 1], st_recv.at[s - 1], x_dev(s)) for s in range(1, NX)
    ]
    for one in stats:
        one.start()
    dqt[...] = jnp.zeros_like(dqt)
    for one in stats:
        one.wait_recv()
    for i in range(NX):
        both = stat[:, i * C : (i + 1) * C]
        for s in range(1, NX):
            j = REL.index((REL[i] + s) % NX)
            both += stat_in[s - 1, :, j * C : (j + 1) * C]
        inverse = 1.0 / both[0:G]
        total[0:G, i * C : (i + 1) * C] = inverse
        total[G : 2 * G, i * C : (i + 1) * C] = both[G : 2 * G] * inverse

    def half(p, core):
        return pl.ds(pl.multiple_of(p * KB + core * C, C), C)

    def to_sibling(p):
        return copy(dkv.at[half(p, 1), :], sib_in.at[p], dc_send.at[p], dc_recv.at[p], c_dev)

    def to_owner(p):
        return copy(z_out.at[p], z_in.at[p], dz_send.at[p], dz_recv.at[p], z_dev(away(p)))

    def finish(p):
        to_sibling(p).wait_recv()
        z_out[p] = (dkv[half(p, 0), :] + sib_in[p]).astype(BF16)
        to_owner(p).start()

    def second(t, carry):
        p = NZ - 1 - t
        rows = pl.ds(pl.multiple_of(p * KB, KB), KB)
        key_sum = jnp.zeros((KB, D), F32)
        val_sum = jnp.zeros((KB, D), F32)
        for h in range(G):
            cols = slice(h * QR, (h + 1) * QR)
            weights = es[rows, cols] * total[h : h + 1, :]
            probs = weights.astype(BF16)
            slopes = (weights * (ds[rows, cols] - total[G + h : G + h + 1, :])).astype(BF16)
            val_sum += dot(probs, qg[:, GD + h * D : GD + (h + 1) * D], NN)
            key_sum += dot(slopes, qg[:, h * D : (h + 1) * D], NN)
            dqt[h] += dot(kt[:, rows], slopes, NN)
        dkv[rows, 0:D] = key_sum
        dkv[rows, D : 2 * D] = val_sum
        to_sibling(p).start()

        @pl.when(t > 0)
        def _():
            finish(p + 1)

        return carry

    lax.fori_loop(0, NZ, second, 0)

    for h in range(G):
        dq_out[:, h * D : (h + 1) * D] = (dqt[h].T * SCALE).astype(BF16)
    dxs = []
    for s in range(1, NX):
        part = dq_out.at[pl.ds(REL.index(s) * C, C), :]
        dxs.append(copy(part, dq_in.at[s - 1], dx_send.at[s - 1], dx_recv.at[s - 1], x_dev(s)))
    for one in dxs:
        one.start()
    for one in dxs:
        one.wait_recv()
    q_sum = dq_out[0:C, :].astype(F32)
    for s in range(1, NX):
        q_sum += dq_in[s - 1].astype(F32)
    q_fin[...] = q_sum.astype(BF16)

    wide = pl.ds(pl.multiple_of(y * GD, GD), GD)
    thin = pl.ds(pl.multiple_of(y * D, D), D)

    def results(s):
        rows = pl.ds(s * U, U)
        return (
            (q_fin.at[rows, :], q_out.at[:, wide]),
            (kv_fin.at[rows, pl.ds(0, D)], k_out.at[:, thin]),
            (kv_fin.at[rows, pl.ds(D, D)], v_out.at[:, thin]),
        )

    outs = []
    for s in range(1, NY):
        for i, (a, b) in enumerate(results(s)):
            outs.append((i, copy(a, b, o_send.at[s - 1, i], o_recv.at[s - 1, i], y_dev(s))))
    mine = [(i, pltpu.make_async_copy(a, b, loc_sem.at[i])) for i, (a, b) in enumerate(results(0))]
    for i, one in outs + mine:
        if i == 0:
            one.start()

    to_sibling(0).wait_recv()
    kv_sum = dkv[0:C, :] + sib_in[0]
    for p in range(NZ - 1, 0, -1):
        to_owner(p).wait_recv()
        kv_sum += z_in[p].astype(F32)
    kv_fin[:, 0:D] = (kv_sum[:, 0:D] * SCALE).astype(BF16)
    kv_fin[:, D : 2 * D] = kv_sum[:, D : 2 * D].astype(BF16)
    for i, one in outs + mine:
        if i > 0:
            one.start()

    for one in [*ys.values(), *xs.values(), *zs.values(), *stats, *dxs]:
        one.wait_send()
    for p in range(NZ):
        c_copy(p).wait_send()
        to_sibling(p).wait_send()
        if p > 0:
            to_owner(p).wait_send()
    for i, one in outs:
        one.wait()
    for i, one in mine:
        one.wait()


def body(queries, keys, values, out_grad, span_order):
    keys_all = NZ * NC * C
    dma = pltpu.SemaphoreType.DMA
    anywhere = pl.BlockSpec(memory_space=pl.ANY)
    return pl.pallas_call(
        kernel,
        out_shape=(
            jax.ShapeDtypeStruct(queries.shape, BF16),
            jax.ShapeDtypeStruct(keys.shape, BF16),
            jax.ShapeDtypeStruct(values.shape, BF16),
        ),
        in_specs=[pl.BlockSpec(memory_space=pltpu.SMEM)] + [anywhere] * 4,
        out_specs=(anywhere,) * 3,
        scratch_shapes=[
            pltpu.VMEM((QR, 2 * GD), BF16),
            pltpu.VMEM((keys_all, 2 * D), BF16),
            pltpu.VMEM((D, keys_all), BF16),
            pltpu.VMEM((keys_all, G * QR), F32),
            pltpu.VMEM((keys_all, G * QR), F32),
            pltpu.VMEM((8, QR), jnp.int32),
            pltpu.VMEM((8, G * QR), F32),
            pltpu.VMEM((8, G * QR), F32),
            pltpu.VMEM((2 * G, QR), F32),
            pltpu.VMEM((NX - 1, 2 * G, QR), F32),
            pltpu.VMEM((2 * G, QR), F32),
            pltpu.VMEM((G, D, QR), F32),
            pltpu.VMEM((keys_all, 2 * D), F32),
            pltpu.VMEM((NZ, C, 2 * D), F32),
            pltpu.VMEM((NZ, C, 2 * D), BF16),
            pltpu.VMEM((NZ, C, 2 * D), BF16),
            pltpu.VMEM((QR, GD), BF16),
            pltpu.VMEM((NX - 1, C, GD), BF16),
            pltpu.VMEM((C, GD), BF16),
            pltpu.VMEM((C, 2 * D), BF16),
            dma((4,)),
            dma((NY - 1, 4)), dma((NY - 1, 4)),
            dma((4, NY)), dma((4, NY)),
            dma((NZ + 1,)), dma((NZ + 1,)),
            dma((NZ,)), dma((NZ,)),
            dma((NX - 1,)), dma((NX - 1,)),
            dma((NZ,)), dma((NZ,)),
            dma((NZ,)), dma((NZ,)),
            dma((NX - 1,)), dma((NX - 1,)),
            dma((NY - 1, 3)), dma((NY - 1, 3)),
        ],
        compiler_params=pltpu.CompilerParams(
            collective_id=0, has_side_effects=True, vmem_limit_bytes=56 * 2**20
        ),
    )(span_order, queries, keys, values, out_grad)


def solution(mesh):
    rows = P(("head", "inner", "outer"), None)
    return jax.shard_map(
        body,
        mesh=mesh,
        in_specs=(rows, rows, rows, rows, P()),
        out_specs=(rows, rows, rows),
        check_vma=False,
    )
```

time: 68.6 us -> 61.5 us (0.90)
  Pallas kernels: 64.6 us -> 57.4 us
    pallas_call x1, Pallas kernels: 64.6 us -> 57.4 us  [body(): pl.pallas_call(kernel, out_shape=(jax.ShapeDtypeStruct(queries.shape, BF1...]
where the time goes in v2:
time: 61.5 us; the launch traced here: 61 us
  Pallas kernels  57.4 us (93%)
  local copies, waits for them, and re-layouts  2.96 us (5%)
  between operations  0.65 us (1%)
    pallas_call x1, Pallas kernels, body(): pl.pallas_call(kernel, out_shape=(jax.ShapeDtypeStruct(queries.shape, BF1...  57.4 us
    unnamed x7, local copies, waits for them, and re-layouts  2.96 us

profile of v2, /device:TPU:32, one launch (start us, length us, event | category | flops | bytes accessed | tf_op | source)
XLA Modules:
  0.0 61.0 jit_solution(15334151303784328186)
XLA Ops:
  0.6 57.4 %shard_map.76 = (bf16[32,2048]{1,0:T(8,128)(2,1)}, bf16[32,512]{1,0:T(8,128)(2,1)}, bf16[32,512]{1,0:T(8,128)(2,1)}) custom-call(s32[256]{0:T(256)} %span.1, bf16[32,2048]{1,0:T(8,128)(2,1)} %q_in.1, bf16[32,512]{1,0:T(8,128)(2,1)} %k_in.1, bf16[32,512]{1,0:T(8,128)(2,1)} %v_in.1, bf16[32,2048]{1,0:T(8,128)(2,1)} %g_in.1), custom_call_target="tpu_custom_call" | custom-call | tf_op jit(solution)/shard_map/pallas_call | solution.py:355
  58.0 0.0 copy-start.1
  58.0 1.6 %copy.11 = bf16[32,2048]{1,0:T(8,128)(2,1)} copy(bf16[32,2048]{1,0:T(8,128)(2,1)} %get-tuple-element.6) | data formatting | bytes 262144
  59.6 0.0 copy-done.1
  59.6 0.0 copy-start
  59.6 0.6 %copy.12 = bf16[32,512]{1,0:T(8,128)(2,1)} copy(bf16[32,512]{1,0:T(8,128)(2,1)S(1)} %copy-done.1) | data formatting | bytes 65536
  60.2 0.2 copy-done
  60.4 0.6 %copy.13 = bf16[32,512]{1,0:T(8,128)(2,1)} copy(bf16[32,512]{1,0:T(8,128)(2,1)S(1)} %copy-done) | data formatting | bytes 65536
Async XLA Ops:
  58.0 1.6 %copy-start.1 = (bf16[32,512]{1,0:T(8,128)(2,1)S(1)}, bf16[32,512]{1,0:T(8,128)(2,1)}, u32[]{:S(2)}) copy-start(bf16[32,512]{1,0:T(8,128)(2,1)} %get-tuple-element.7) | copy-start | bytes 98308
  59.6 0.8 %copy-start = (bf16[32,512]{1,0:T(8,128)(2,1)S(1)}, bf16[32,512]{1,0:T(8,128)(2,1)}, u32[]{:S(2)}) copy-start(bf16[32,512]{1,0:T(8,128)(2,1)} %get-tuple-element.8) | copy-start | bytes 98308

commit v3 on v2

--- a/solution.py
+++ b/solution.py
@@ -29,7 +29,7 @@
 
 
 def kernel(
-    span, q_in, k_in, v_in, g_in, q_out, k_out, v_out,
+    span, q_in, k_in, v_in, g_in, q_parts, kv_parts,
     qg, kv, kt, es, ds, qp, nsum, wsum, stat, stat_in, total, dqt, dkv, sib_in, z_out, z_in,
     dq_out, dq_in, q_fin, kv_fin,
     loc_sem, y_send, y_recv, x_send, x_recv, z_send, z_recv, c_send, c_recv,
@@ -82,7 +82,7 @@
     barrier = pltpu.get_barrier_semaphore()
     partners = (
         [y_dev(s) for s in range(1, NY)] + [x_dev(s) for s in range(1, NX)]
-        + [z_dev(s) for s in range(1, NZ)] + [c_dev]
+        + [z_dev(s) for s in (1, -1, 2, -2)] + [c_dev]
     )
     for device in partners:
         pl.semaphore_signal(barrier, inc=1, device_id=device, device_id_type=MESH)
@@ -176,9 +176,6 @@
         xs[2, s].start()
         xs[1, s].wait_recv()
         xs[3, s].start()
-    for i in (6, 5):
-        zs[i].wait_recv()
-        c_copy(i).start()
 
     row = lax.broadcasted_iota(jnp.int32, (U, 1), 0)
 
@@ -193,8 +190,6 @@
                 unit = up(y, NY, s) * (NZ * NX * NC) + (zz % 2) * (NZ // 2 * NX * NC) + ((zz // 2) * NX + x) * NC + cc
                 masks.append(row + span[unit] * U <= limit)
         mask = jnp.concatenate(masks, axis=0)
-        if low == 0:
-            kt[:, rows] = keys.T
         for h in range(G):
             cols = slice(h * QR + low, h * QR + low + width)
             scores = dot(keys, qg[low : low + width, h * D : (h + 1) * D], NT)
@@ -206,6 +201,12 @@
             wsum[:, cols] += jnp.sum((raised * grads).reshape(KB // 8, 8, width), axis=0)
 
     def near(p, carry):
+        @pl.when(p == 2)
+        def _():
+            for i in (6, 5):
+                zs[i].wait_recv()
+                c_copy(i).start()
+
         @pl.when(p > 0)
         def _():
             c_copy(p).wait_recv()
@@ -214,14 +215,17 @@
         return carry
 
     def far(p, carry):
+        @pl.when(p == 1)
+        def _():
+            zs[7].wait_recv()
+            zs[8].wait_recv()
+            c_copy(7).start()
+
         tile(p, QR // 2, QR // 2)
         return carry
 
     c_copy(0).wait_recv()
     lax.fori_loop(0, NZ - 1, near, 0)
-    zs[7].wait_recv()
-    zs[8].wait_recv()
-    c_copy(7).start()
     for s in range(NY):
         xs[2, s].wait_recv()
         xs[3, s].wait_recv()
@@ -239,6 +243,8 @@
     for one in stats:
         one.start()
     dqt[...] = jnp.zeros_like(dqt)
+    for p in range(NZ):
+        kt[:, p * KB : (p + 1) * KB] = kv[p * KB : (p + 1) * KB, 0:D].T
     for one in stats:
         one.wait_recv()
     for i in range(NX):
@@ -256,20 +262,35 @@
     def to_sibling(p):
         return copy(dkv.at[half(p, 1), :], sib_in.at[p], dc_send.at[p], dc_recv.at[p], c_dev)
 
-    def to_owner(p):
-        return copy(z_out.at[p], z_in.at[p], dz_send.at[p], dz_recv.at[p], z_dev(away(p)))
+    def z_sum(i, p, step, first, width):
+        cols = pl.ds(first, width)
+        return copy(z_out.at[p, :, cols], z_in.at[p, :, cols], dz_send.at[i], dz_recv.at[i], z_dev(step))
+
+    zsums = {
+        7: z_sum(7, 7, 2, 0, D), 8: z_sum(8, 7, -2, D, D),
+        6: z_sum(6, 6, -1, 0, 2 * D), 5: z_sum(5, 5, 1, 0, 2 * D),
+        4: z_sum(4, 4, -2, 0, 2 * D), 3: z_sum(3, 3, 2, 0, 2 * D),
+        2: z_sum(2, 2, -1, 0, 2 * D), 1: z_sum(1, 1, 1, 0, 2 * D),
+    }
 
     def finish(p):
         to_sibling(p).wait_recv()
         z_out[p] = (dkv[half(p, 0), :] + sib_in[p]).astype(BF16)
-        to_owner(p).start()
-
-    def second(t, carry):
-        p = NZ - 1 - t
-        rows = pl.ds(pl.multiple_of(p * KB, KB), KB)
+
+    def relay(p, nearer, part, first):
+        to_sibling(p).wait_recv()
+        zsums[nearer].wait_recv()
+        zsums[part].wait_recv()
+        both = dkv[half(p, 0), :] + sib_in[p] + z_in[nearer].astype(F32)
+        cols, rest = slice(first, first + D), slice(D - first, 2 * D - first)
+        z_out[p, :, cols] = (both[:, cols] + z_in[7, :, cols].astype(F32)).astype(BF16)
+        z_out[p, :, rest] = both[:, rest].astype(BF16)
+        zsums[p].start()
+
+    def sums(p, heads, rows):
         key_sum = jnp.zeros((KB, D), F32)
         val_sum = jnp.zeros((KB, D), F32)
-        for h in range(G):
+        for h in heads:
             cols = slice(h * QR, (h + 1) * QR)
             weights = es[rows, cols] * total[h : h + 1, :]
             probs = weights.astype(BF16)
@@ -277,90 +298,125 @@
             val_sum += dot(probs, qg[:, GD + h * D : GD + (h + 1) * D], NN)
             key_sum += dot(slopes, qg[:, h * D : (h + 1) * D], NN)
             dqt[h] += dot(kt[:, rows], slopes, NN)
-        dkv[rows, 0:D] = key_sum
-        dkv[rows, D : 2 * D] = val_sum
+        return key_sum, val_sum
+
+    def block(p):
+        return pl.ds(pl.multiple_of(p * KB, KB), KB)
+
+    def second(t, carry):
+        p = NZ - 1 - t
+        rows = block(p)
+        dkv[rows, 0:D], dkv[rows, D : 2 * D] = sums(p, range(0, G // 2), rows)
+        return carry
+
+    def third(t, carry):
+        p = NZ - 1 - t
+        rows = block(p)
+        key_sum, val_sum = sums(p, range(G // 2, G), rows)
+        dkv[rows, 0:D] += key_sum
+        dkv[rows, D : 2 * D] += val_sum
         to_sibling(p).start()
 
-        @pl.when(t > 0)
+        @pl.when((p == 5) | (p == 4) | (p == 3) | (p == 0))
         def _():
-            finish(p + 1)
+            finish(p + 2)
+
+        @pl.when(p == 5)
+        def _():
+            zsums[7].start()
+            zsums[8].start()
+
+        for q in (6, 5, 2):
+
+            @pl.when(p == q - 2)
+            def _(q=q):
+                zsums[q].start()
 
         return carry
 
+    def q_sums(half):
+        cols = pl.ds(half * GD // 2, GD // 2)
+        for h in range(half * G // 2, (half + 1) * G // 2):
+            dq_out[:, h * D : (h + 1) * D] = (dqt[h].T * SCALE).astype(BF16)
+        copies = []
+        for s in (2, 1, 3):
+            part = dq_out.at[pl.ds(REL.index(s) * C, C), cols]
+            i = half * NX + s
+            copies.append(copy(part, dq_in.at[s - 1, :, cols], dx_send.at[i], dx_recv.at[i], x_dev(s)))
+        for one in copies:
+            one.start()
+        return copies
+
+    def to_tokens(i, src, dst):
+        copies = [pltpu.make_async_copy(src.at[pl.ds(0, U), :], dst, loc_sem.at[i])]
+        for s in range(1, NY):
+            copies.append(copy(src.at[pl.ds(s * U, U), :], dst, o_send.at[i, s], o_recv.at[i, s], y_dev(s)))
+        for one in copies:
+            one.start()
+        return copies
+
+    def q_done(half, copies):
+        cols = slice(half * GD // 2, (half + 1) * GD // 2)
+        for one in copies:
+            one.wait_recv()
+        q_sum = dq_out[0:C, cols].astype(F32)
+        for s in range(1, NX):
+            q_sum += dq_in[s - 1, :, cols].astype(F32)
+        q_fin[half] = q_sum.astype(BF16)
+        return to_tokens(half, q_fin.at[half], q_parts.at[y, half])
+
     lax.fori_loop(0, NZ, second, 0)
-
-    for h in range(G):
-        dq_out[:, h * D : (h + 1) * D] = (dqt[h].T * SCALE).astype(BF16)
-    dxs = []
-    for s in range(1, NX):
-        part = dq_out.at[pl.ds(REL.index(s) * C, C), :]
-        dxs.append(copy(part, dq_in.at[s - 1], dx_send.at[s - 1], dx_recv.at[s - 1], x_dev(s)))
-    for one in dxs:
-        one.start()
-    for one in dxs:
-        one.wait_recv()
-    q_sum = dq_out[0:C, :].astype(F32)
-    for s in range(1, NX):
-        q_sum += dq_in[s - 1].astype(F32)
-    q_fin[...] = q_sum.astype(BF16)
-
-    wide = pl.ds(pl.multiple_of(y * GD, GD), GD)
-    thin = pl.ds(pl.multiple_of(y * D, D), D)
-
-    def results(s):
-        rows = pl.ds(s * U, U)
-        return (
-            (q_fin.at[rows, :], q_out.at[:, wide]),
-            (kv_fin.at[rows, pl.ds(0, D)], k_out.at[:, thin]),
-            (kv_fin.at[rows, pl.ds(D, D)], v_out.at[:, thin]),
-        )
-
-    outs = []
-    for s in range(1, NY):
-        for i, (a, b) in enumerate(results(s)):
-            outs.append((i, copy(a, b, o_send.at[s - 1, i], o_recv.at[s - 1, i], y_dev(s))))
-    mine = [(i, pltpu.make_async_copy(a, b, loc_sem.at[i])) for i, (a, b) in enumerate(results(0))]
-    for i, one in outs + mine:
-        if i == 0:
-            one.start()
-
+    low_sums = q_sums(0)
+    lax.fori_loop(0, NZ, third, 0)
+    high_sums = q_sums(1)
+    finish(1)
+    zsums[1].start()
+    relay(4, 6, 8, D)
+    relay(3, 5, 7, 0)
+    outs = q_done(0, low_sums)
     to_sibling(0).wait_recv()
     kv_sum = dkv[0:C, :] + sib_in[0]
-    for p in range(NZ - 1, 0, -1):
-        to_owner(p).wait_recv()
+    for p in (1, 2):
+        zsums[p].wait_recv()
+        kv_sum += z_in[p].astype(F32)
+    outs += q_done(1, high_sums)
+    for p in (3, 4):
+        zsums[p].wait_recv()
         kv_sum += z_in[p].astype(F32)
     kv_fin[:, 0:D] = (kv_sum[:, 0:D] * SCALE).astype(BF16)
     kv_fin[:, D : 2 * D] = kv_sum[:, D : 2 * D].astype(BF16)
-    for i, one in outs + mine:
-        if i > 0:
-            one.start()
-
-    for one in [*ys.values(), *xs.values(), *zs.values(), *stats, *dxs]:
+    outs += to_tokens(2, kv_fin, kv_parts.at[y])
+
+    for one in [*ys.values(), *xs.values(), *zs.values(), *zsums.values(), *stats, *low_sums, *high_sums]:
         one.wait_send()
     for p in range(NZ):
         c_copy(p).wait_send()
         to_sibling(p).wait_send()
-        if p > 0:
-            to_owner(p).wait_send()
-    for i, one in outs:
+    for one in outs:
         one.wait()
-    for i, one in mine:
-        one.wait()
+
+
+def last_columns(q_parts, kv_parts, q_out, k_out, v_out):
+    for h in range(NY):
+        for half in range(2):
+            first = h * GD + half * GD // 2
+            q_out[:, first : first + GD // 2] = q_parts[h, half]
+        k_out[:, h * D : (h + 1) * D] = kv_parts[h, :, 0:D]
+        v_out[:, h * D : (h + 1) * D] = kv_parts[h, :, D : 2 * D]
 
 
 def body(queries, keys, values, out_grad, span_order):
     keys_all = NZ * NC * C
     dma = pltpu.SemaphoreType.DMA
     anywhere = pl.BlockSpec(memory_space=pl.ANY)
-    return pl.pallas_call(
+    parts = pl.pallas_call(
         kernel,
         out_shape=(
-            jax.ShapeDtypeStruct(queries.shape, BF16),
-            jax.ShapeDtypeStruct(keys.shape, BF16),
-            jax.ShapeDtypeStruct(values.shape, BF16),
+            jax.ShapeDtypeStruct((NY, 2, U, GD // 2), BF16),
+            jax.ShapeDtypeStruct((NY, U, 2 * D), BF16),
         ),
         in_specs=[pl.BlockSpec(memory_space=pltpu.SMEM)] + [anywhere] * 4,
-        out_specs=(anywhere,) * 3,
+        out_specs=(anywhere,) * 2,
         scratch_shapes=[
             pltpu.VMEM((QR, 2 * GD), BF16),
             pltpu.VMEM((keys_all, 2 * D), BF16),
@@ -380,7 +436,7 @@
             pltpu.VMEM((NZ, C, 2 * D), BF16),
             pltpu.VMEM((QR, GD), BF16),
             pltpu.VMEM((NX - 1, C, GD), BF16),
-            pltpu.VMEM((C, GD), BF16),
+            pltpu.VMEM((2, C, GD // 2), BF16),
             pltpu.VMEM((C, 2 * D), BF16),
             dma((4,)),
             dma((NY - 1, 4)), dma((NY - 1, 4)),
@@ -389,14 +445,22 @@
             dma((NZ,)), dma((NZ,)),
             dma((NX - 1,)), dma((NX - 1,)),
             dma((NZ,)), dma((NZ,)),
-            dma((NZ,)), dma((NZ,)),
-            dma((NX - 1,)), dma((NX - 1,)),
-            dma((NY - 1, 3)), dma((NY - 1, 3)),
+            dma((NZ + 1,)), dma((NZ + 1,)),
+            dma((2 * NX,)), dma((2 * NX,)),
+            dma((3, NY)), dma((3, NY)),
         ],
         compiler_params=pltpu.CompilerParams(
             collective_id=0, has_side_effects=True, vmem_limit_bytes=56 * 2**20
         ),
     )(span_order, queries, keys, values, out_grad)
+    return pl.pallas_call(
+        last_columns,
+        out_shape=(
+            jax.ShapeDtypeStruct(queries.shape, BF16),
+            jax.ShapeDtypeStruct(keys.shape, BF16),
+            jax.ShapeDtypeStruct(values.shape, BF16),
+        ),
+    )(*parts)
 
 
 def solution(mesh):

time: 61.5 us -> 59.5 us (0.967)
  the two profiles are of different devices: /device:TPU:32 before, /device:TPU:1 now
where the time goes in v3:
time: 59.5 us; the launch traced here: 59.3 us
  Pallas kernels  58.6 us (98%)
  between operations  0.64 us (1%)
    pallas_call x1, Pallas kernels, body(): pl.pallas_call(kernel, out_shape=(jax.ShapeDtypeStruct((NY, 2, U, GD // 2...  57.1 us
    pallas_call x1, Pallas kernels, body(): pl.pallas_call(last_columns, out_shape=(jax.ShapeDtypeStruct(queries.shap...  1.58 us

profile of v3, /device:TPU:1, one launch (start us, length us, event | category | flops | bytes accessed | tf_op | source)
XLA Modules:
  0.0 59.3 jit_solution(12017135751995656032)
XLA Ops:
  0.6 57.1 %shard_map.76 = (bf16[4,2,32,256]{3,2,1,0:T(8,128)(2,1)}, bf16[4,32,256]{2,1,0:T(8,128)(2,1)}) custom-call(s32[256]{0:T(256)} %span.1, bf16[32,2048]{1,0:T(8,128)(2,1)} %q_in.1, bf16[32,512]{1,0:T(8,128)(2,1)} %k_in.1, bf16[32,512]{1,0:T(8,128)(2,1)} %v_in.1, bf16[32,2048]{1,0:T(8,128)(2,1)} %g_in.1), custom_call_target="tpu_custom_call" | custom-call | tf_op jit(solution)/shard_map/pallas_call | solution.py:412
  57.7 1.6 %shard_map.77 = (bf16[32,2048]{1,0:T(8,128)(2,1)}, bf16[32,512]{1,0:T(8,128)(2,1)}, bf16[32,512]{1,0:T(8,128)(2,1)}) custom-call(bf16[4,2,32,256]{3,2,1,0:T(8,128)(2,1)} %get-tuple-element.5.q_parts, bf16[4,32,256]{2,1,0:T(8,128)(2,1)} %get-tuple-element.6.kv_parts), custom_call_target="tpu_custom_call" | custom-call | tf_op jit(solution)/shard_map/pallas_call | solution.py:456

commit v4 on v3

--- a/solution.py
+++ b/solution.py
@@ -152,6 +152,10 @@
     for i in (2, 1, 4, 3):
         zs[i].start()
     c_copy(0).start()
+    xs[0, 0].wait_recv()
+    xs[2, 0].start()
+    xs[1, 0].wait_recv()
+    xs[3, 0].start()
     for s in order[1:]:
         ys[s, 2].wait_recv()
         ys[s, 3].wait_recv()
@@ -161,10 +165,6 @@
         zs[i].wait_recv()
         zs[i + 4].start()
         c_copy(i).start()
-    xs[0, 0].wait_recv()
-    xs[2, 0].start()
-    xs[1, 0].wait_recv()
-    xs[3, 0].start()
     zs[4].wait_recv()
     zs[7].start()
     c_copy(4).start()
@@ -179,16 +179,17 @@
 
     row = lax.broadcasted_iota(jnp.int32, (U, 1), 0)
 
-    def tile(p, low, width):
-        rows = pl.ds(p * KB if isinstance(p, int) else pl.multiple_of(p * KB, KB), KB)
+    def tile(p, count, low, width):
+        rows = pl.ds(p * KB if isinstance(p, int) else pl.multiple_of(p * KB, KB), count * KB)
         keys, vals = kv[rows, 0:D], kv[rows, D : 2 * D]
         masks = []
         limit = jnp.broadcast_to(qp[0:1, low : low + width], (U, width))
-        zz = up(z, NZ, away(p))
-        for cc in (c, 1 - c):
-            for s in range(NY):
-                unit = up(y, NY, s) * (NZ * NX * NC) + (zz % 2) * (NZ // 2 * NX * NC) + ((zz // 2) * NX + x) * NC + cc
-                masks.append(row + span[unit] * U <= limit)
+        for i in range(count):
+            zz = up(z, NZ, away(p + i))
+            for cc in (c, 1 - c):
+                for s in range(NY):
+                    unit = up(y, NY, s) * (NZ * NX * NC) + (zz % 2) * (NZ // 2 * NX * NC) + ((zz // 2) * NX + x) * NC + cc
+                    masks.append(row + span[unit] * U <= limit)
         mask = jnp.concatenate(masks, axis=0)
         for h in range(G):
             cols = slice(h * QR + low, h * QR + low + width)
@@ -197,41 +198,41 @@
             grads = dot(vals, qg[low : low + width, GD + h * D : GD + (h + 1) * D], NT)
             es[rows, cols] = raised
             ds[rows, cols] = grads
-            nsum[:, cols] += jnp.sum(raised.reshape(KB // 8, 8, width), axis=0)
-            wsum[:, cols] += jnp.sum((raised * grads).reshape(KB // 8, 8, width), axis=0)
-
-    def near(p, carry):
-        @pl.when(p == 2)
+            nsum[:, cols] += jnp.sum(raised.reshape(count * KB // 8, 8, width), axis=0)
+            wsum[:, cols] += jnp.sum((raised * grads).reshape(count * KB // 8, 8, width), axis=0)
+
+    def near(t, carry):
+        @pl.when(t == 1)
         def _():
             for i in (6, 5):
                 zs[i].wait_recv()
                 c_copy(i).start()
 
-        @pl.when(p > 0)
-        def _():
-            c_copy(p).wait_recv()
-
-        tile(p, 0, QR // 2)
+        c_copy(2 * t).wait_recv()
+        c_copy(2 * t + 1).wait_recv()
+        tile(2 * t, 2, 0, QR // 2)
         return carry
 
-    def far(p, carry):
-        @pl.when(p == 1)
+    def far(t, carry):
+        @pl.when(t == 1)
         def _():
             zs[7].wait_recv()
             zs[8].wait_recv()
             c_copy(7).start()
 
-        tile(p, QR // 2, QR // 2)
+        tile(2 * t, 2, QR // 2, QR // 2)
         return carry
 
-    c_copy(0).wait_recv()
-    lax.fori_loop(0, NZ - 1, near, 0)
+    lax.fori_loop(0, 3, near, 0)
+    c_copy(6).wait_recv()
+    tile(6, 1, 0, QR // 2)
     for s in range(NY):
         xs[2, s].wait_recv()
         xs[3, s].wait_recv()
-    lax.fori_loop(0, NZ - 1, far, 0)
+    lax.fori_loop(0, 3, far, 0)
     c_copy(7).wait_recv()
-    tile(7, 0, QR)
+    tile(6, 2, QR // 2, QR // 2)
+    tile(7, 1, 0, QR // 2)
 
     for h in range(G):
         cols = slice(h * QR, (h + 1) * QR)
@@ -287,9 +288,9 @@
         z_out[p, :, rest] = both[:, rest].astype(BF16)
         zsums[p].start()
 
-    def sums(p, heads, rows):
-        key_sum = jnp.zeros((KB, D), F32)
-        val_sum = jnp.zeros((KB, D), F32)
+    def sums(heads, rows):
+        key_sum = jnp.zeros((2 * KB, D), F32)
+        val_sum = jnp.zeros((2 * KB, D), F32)
         for h in heads:
             cols = slice(h * QR, (h + 1) * QR)
             weights = es[rows, cols] * total[h : h + 1, :]
@@ -300,37 +301,39 @@
             dqt[h] += dot(kt[:, rows], slopes, NN)
         return key_sum, val_sum
 
-    def block(p):
-        return pl.ds(pl.multiple_of(p * KB, KB), KB)
+    def blocks(t):
+        return pl.ds(pl.multiple_of((NZ - 2 - 2 * t) * KB, 2 * KB), 2 * KB)
 
     def second(t, carry):
-        p = NZ - 1 - t
-        rows = block(p)
-        dkv[rows, 0:D], dkv[rows, D : 2 * D] = sums(p, range(0, G // 2), rows)
+        rows = blocks(t)
+        dkv[rows, 0:D], dkv[rows, D : 2 * D] = sums(range(0, G // 2), rows)
         return carry
 
     def third(t, carry):
-        p = NZ - 1 - t
-        rows = block(p)
-        key_sum, val_sum = sums(p, range(G // 2, G), rows)
+        rows = blocks(t)
+        key_sum, val_sum = sums(range(G // 2, G), rows)
         dkv[rows, 0:D] += key_sum
         dkv[rows, D : 2 * D] += val_sum
-        to_sibling(p).start()
-
-        @pl.when((p == 5) | (p == 4) | (p == 3) | (p == 0))
+        to_sibling(NZ - 1 - 2 * t).start()
+        to_sibling(NZ - 2 - 2 * t).start()
+
+        @pl.when(t == 1)
         def _():
-            finish(p + 2)
-
-        @pl.when(p == 5)
-        def _():
+            finish(7)
             zsums[7].start()
             zsums[8].start()
-
-        for q in (6, 5, 2):
-
-            @pl.when(p == q - 2)
-            def _(q=q):
-                zsums[q].start()
+            finish(6)
+            zsums[6].start()
+
+        @pl.when(t == 2)
+        def _():
+            finish(5)
+            zsums[5].start()
+
+        @pl.when(t == 3)
+        def _():
+            finish(2)
+            zsums[2].start()
 
         return carry
 
@@ -365,9 +368,9 @@
         q_fin[half] = q_sum.astype(BF16)
         return to_tokens(half, q_fin.at[half], q_parts.at[y, half])
 
-    lax.fori_loop(0, NZ, second, 0)
+    lax.fori_loop(0, NZ // 2, second, 0)
     low_sums = q_sums(0)
-    lax.fori_loop(0, NZ, third, 0)
+    lax.fori_loop(0, NZ // 2, third, 0)
     high_sums = q_sums(1)
     finish(1)
     zsums[1].start()

time: 59.5 us -> 56.4 us (0.948)
  the two profiles are of different devices: /device:TPU:1 before, /device:TPU:32 now
where the time goes in v4:
time: 56.4 us; the launch traced here: 56.2 us
  Pallas kernels  55.6 us (99%)
  between operations  0.64 us (1%)
    pallas_call x1, Pallas kernels, body(): pl.pallas_call(kernel, out_shape=(jax.ShapeDtypeStruct((NY, 2, U, GD // 2...  54 us
    pallas_call x1, Pallas kernels, body(): pl.pallas_call(last_columns, out_shape=(jax.ShapeDtypeStruct(queries.shap...  1.58 us

profile of v4, /device:TPU:32, one launch (start us, length us, event | category | flops | bytes accessed | tf_op | source)
XLA Modules:
  0.0 56.2 jit_solution(6673774717354728931)
XLA Ops:
  0.6 54.0 %shard_map.76 = (bf16[4,2,32,256]{3,2,1,0:T(8,128)(2,1)}, bf16[4,32,256]{2,1,0:T(8,128)(2,1)}) custom-call(s32[256]{0:T(256)} %span.1, bf16[32,2048]{1,0:T(8,128)(2,1)} %q_in.1, bf16[32,512]{1,0:T(8,128)(2,1)} %k_in.1, bf16[32,512]{1,0:T(8,128)(2,1)} %v_in.1, bf16[32,2048]{1,0:T(8,128)(2,1)} %g_in.1), custom_call_target="tpu_custom_call" | custom-call | tf_op jit(solution)/shard_map/pallas_call | solution.py:415
  54.7 1.6 %shard_map.77 = (bf16[32,2048]{1,0:T(8,128)(2,1)}, bf16[32,512]{1,0:T(8,128)(2,1)}, bf16[32,512]{1,0:T(8,128)(2,1)}) custom-call(bf16[4,2,32,256]{3,2,1,0:T(8,128)(2,1)} %get-tuple-element.5.q_parts, bf16[4,32,256]{2,1,0:T(8,128)(2,1)} %get-tuple-element.6.kv_parts), custom_call_target="tpu_custom_call" | custom-call | tf_op jit(solution)/shard_map/pallas_call | solution.py:459

commit v5 on v4

--- a/solution.py
+++ b/solution.py
@@ -288,9 +288,9 @@
         z_out[p, :, rest] = both[:, rest].astype(BF16)
         zsums[p].start()
 
-    def sums(heads, rows):
-        key_sum = jnp.zeros((2 * KB, D), F32)
-        val_sum = jnp.zeros((2 * KB, D), F32)
+    def sums(heads, rows, count):
+        key_sum = jnp.zeros((count * KB, D), F32)
+        val_sum = jnp.zeros((count * KB, D), F32)
         for h in heads:
             cols = slice(h * QR, (h + 1) * QR)
             weights = es[rows, cols] * total[h : h + 1, :]
@@ -305,13 +305,13 @@
         return pl.ds(pl.multiple_of((NZ - 2 - 2 * t) * KB, 2 * KB), 2 * KB)
 
     def second(t, carry):
-        rows = blocks(t)
-        dkv[rows, 0:D], dkv[rows, D : 2 * D] = sums(range(0, G // 2), rows)
+        rows = pl.ds(pl.multiple_of(t * 4 * KB, 4 * KB), 4 * KB)
+        dkv[rows, 0:D], dkv[rows, D : 2 * D] = sums(range(0, G // 2), rows, 4)
         return carry
 
     def third(t, carry):
         rows = blocks(t)
-        key_sum, val_sum = sums(range(G // 2, G), rows)
+        key_sum, val_sum = sums(range(G // 2, G), rows, 2)
         dkv[rows, 0:D] += key_sum
         dkv[rows, D : 2 * D] += val_sum
         to_sibling(NZ - 1 - 2 * t).start()
@@ -368,7 +368,7 @@
         q_fin[half] = q_sum.astype(BF16)
         return to_tokens(half, q_fin.at[half], q_parts.at[y, half])
 
-    lax.fori_loop(0, NZ // 2, second, 0)
+    lax.fori_loop(0, NZ // 4, second, 0)
     low_sums = q_sums(0)
     lax.fori_loop(0, NZ // 2, third, 0)
     high_sums = q_sums(1)

time: 56.4 us -> 56.1 us (level)
  no operation moved by 1% of the time
where the time goes in v5:
time: 56.1 us; the launch traced here: 55.9 us
  Pallas kernels  55.3 us (99%)
  between operations  0.64 us (1%)
    pallas_call x1, Pallas kernels, body(): pl.pallas_call(kernel, out_shape=(jax.ShapeDtypeStruct((NY, 2, U, GD // 2...  53.7 us
    pallas_call x1, Pallas kernels, body(): pl.pallas_call(last_columns, out_shape=(jax.ShapeDtypeStruct(queries.shap...  1.58 us

profile of v5, /device:TPU:32, one launch (start us, length us, event | category | flops | bytes accessed | tf_op | source)
XLA Modules:
  0.0 55.9 jit_solution(5591329635397353017)
XLA Ops:
  0.6 53.7 %shard_map.76 = (bf16[4,2,32,256]{3,2,1,0:T(8,128)(2,1)}, bf16[4,32,256]{2,1,0:T(8,128)(2,1)}) custom-call(s32[256]{0:T(256)} %span.1, bf16[32,2048]{1,0:T(8,128)(2,1)} %q_in.1, bf16[32,512]{1,0:T(8,128)(2,1)} %k_in.1, bf16[32,512]{1,0:T(8,128)(2,1)} %v_in.1, bf16[32,2048]{1,0:T(8,128)(2,1)} %g_in.1), custom_call_target="tpu_custom_call" | custom-call | tf_op jit(solution)/shard_map/pallas_call | solution.py:415
  54.3 1.6 %shard_map.77 = (bf16[32,2048]{1,0:T(8,128)(2,1)}, bf16[32,512]{1,0:T(8,128)(2,1)}, bf16[32,512]{1,0:T(8,128)(2,1)}) custom-call(bf16[4,2,32,256]{3,2,1,0:T(8,128)(2,1)} %get-tuple-element.5.q_parts, bf16[4,32,256]{2,1,0:T(8,128)(2,1)} %get-tuple-element.6.kv_parts), custom_call_target="tpu_custom_call" | custom-call | tf_op jit(solution)/shard_map/pallas_call | solution.py:459
